TPU v7x, 128 devices: a whole 4x4x4 slice. The times are simulated.
128 devices in a mesh: fft: 64 (over y_hi, x, z, core), grp: 2 (over y_lo).
Axes of the slice: x: 4, y: 4 (y_hi: 2, y_lo: 2; y = y_hi * 2 + y_lo), z: 4, core: 2. Of those that a mesh axis runs over, the one named last changes fastest.
Arguments:
- limbs_a: int32 [4096, 8192], P(('fft', 'grp')), may hold values from -128 to 127
- limbs_b: int32 [4096, 8192], P(('fft', 'grp')), may hold values from -128 to 127
Outputs:
- product: float32 [4096, 16384], P(('fft', 'grp'))
All inputs are finite; a program needn't handle non-finite values.
Results may differ from a plain program's by a relative error of at most 0.000098.
Values sent between devices are 32-bit elements; how exact they have to be, the bound alone decides.
A program may use at most 128 MiB of HBM per device.

v0:
```python
import functools
import math

import jax
import jax.numpy as jnp
import ml_dtypes
import numpy as np
from jax import lax
from jax.experimental import pallas as pl
from jax.experimental.pallas import tpu as pltpu
from jax.sharding import PartitionSpec as P

MESH = pl.DeviceIdType.MESH
ROWS = 16384
COLS = 4096
TOTAL = ROWS * COLS
DIGIT_VAR = 5461.25
DEV = 128
LOCAL = COLS // DEV
FWD_CHUNKS = 4
INV_CHUNKS = 2
F32 = jnp.float32
BF16 = jnp.bfloat16


def turn(num, den):
    angle = (np.asarray(num, np.int64) % den) * (2.0 * math.pi / den)
    return np.cos(angle), np.sin(angle)


def split_pair(table):
    high = table.astype(ml_dtypes.bfloat16)
    low = (table - high.astype(np.float64)).astype(ml_dtypes.bfloat16)
    return high, low


@functools.lru_cache(None)
def matrix_tables():
    ka = np.arange(128)
    lane = np.arange(64)
    order = np.concatenate([2 * np.arange(64), 2 * np.arange(64) + 1])
    c, s = turn(np.outer(2 * ka + 1, order), 512)
    first = split_pair(np.concatenate([c, -s], 0))
    first = np.concatenate([first[0], first[1]], 1)
    c, s = turn(np.outer(lane, lane), 64)
    z = np.zeros_like(c)
    c2, s2 = np.block([[c, z], [z, c]]), np.block([[s, z], [z, s]])
    lanes_fwd = split_pair(np.block([[c2, -s2], [s2, c2]]))
    lanes_inv = split_pair(np.block([[c2, s2], [-s2, c2]]))
    c, s = turn(np.outer(ka, ka), 128)
    dev_fwd = split_pair(np.block([[c, s], [-s, c]]))
    dev_inv = split_pair(np.block([[c, -s], [s, c]]))
    scale = 2.0 / (TOTAL * DIGIT_VAR * math.sqrt(TOTAL // 2))
    order = np.concatenate([2 * np.arange(128), 2 * np.arange(128) + 1])
    c, s = turn(np.outer(order, 2 * ka + 1), 512)
    last = split_pair(np.concatenate([c, -s], 1) * scale)
    mats = [first, *lanes_fwd, *dev_fwd, *dev_inv, *lanes_inv, *last]
    return np.stack(mats)


@functools.lru_cache(None)
def vector_tables():
    ka = np.arange(128)[:, None]
    lane = np.arange(128)[None, :]
    low, par = lane % 64, lane // 64
    zero = 0 * lane
    k1 = ka + 256 * low
    pairs = [
        turn(-low * (2 * ka + 1), 2 * ROWS),
        turn(-(2 * k1 + 1), 2 * TOTAL),
        turn(-ka + zero, COLS),
        turn(ka * par, COLS),
        turn(2 * ka + zero, COLS),
        turn(2 * (2 * k1 + 1), 2 * TOTAL),
        turn(par * (2 * k1 + 1), 2 * TOTAL),
        turn(np.arange(128)[:, None] % 16 * par, 32),
    ]
    return np.stack([t for pair in pairs for t in pair]).astype(np.float32)


def times(a, b):
    return a[0] * b[0] - a[1] * b[1], a[0] * b[1] + a[1] * b[0]


def turned(value, num, den):
    num %= den
    re, im = value
    if num == 0:
        return value
    if 4 * num == den:
        return -im, re
    if 2 * num == den:
        return -re, -im
    if 4 * num == 3 * den:
        return im, -re
    c, s = math.cos(2 * math.pi * num / den), math.sin(2 * math.pi * num / den)
    if 8 * num % den == 0:
        root = math.sqrt(0.5)
        sc, ss = math.copysign(1.0, c), math.copysign(1.0, s)
        first = re if sc > 0 else -re
        first = first - im if ss > 0 else first + im
        second = re if ss > 0 else -re
        second = second + im if sc > 0 else second - im
        return first * root, second * root
    return re * c - im * s, re * s + im * c


def small_dft(values, sign):
    n = len(values)
    if n == 1:
        return values
    half = n // 2
    even = [(a[0] + b[0], a[1] + b[1]) for a, b in zip(values[:half], values[half:])]
    odd = [
        turned((a[0] - b[0], a[1] - b[1]), sign * i, n)
        for i, (a, b) in enumerate(zip(values[:half], values[half:]))
    ]
    even, odd = small_dft(even, sign), small_dft(odd, sign)
    return [v for pair in zip(even, odd) for v in pair]


def halves(value):
    high = value.astype(BF16)
    return high, (value - high.astype(F32)).astype(BF16)


def dot(a, b):
    return jnp.dot(a, b, preferred_element_type=F32)


def kernel(
    a_hbm, b_hbm, mats_hbm, vecs_hbm, out_hbm,
    a_ref, b_ref, mats, vecs, out_ref, sent, got, mid, quot, back, home, turn_f, turn_d,
    in_sem, out_sem, send_f, recv_f, send_i, recv_i,
):
    me = lax.axis_index("fft") * 2 + lax.axis_index("grp")
    barrier = pltpu.get_barrier_semaphore()

    loads = [
        pltpu.make_async_copy(src, dst, in_sem.at[i])
        for i, (src, dst) in enumerate(
            ((a_hbm, a_ref), (b_hbm, b_ref), (mats_hbm, mats), (vecs_hbm, vecs))
        )
    ]
    for load in loads:
        load.start()

    def greet(step, _):
        peer = lax.rem(me + step, DEV)
        pl.semaphore_signal(
            barrier, inc=1, device_id=(peer // 2, lax.rem(peer, 2)), device_id_type=MESH
        )
        return 0

    lax.fori_loop(1, DEV, greet, 0)

    def peer_at(step):
        mixed = lax.rem(step * 37, DEV)
        core = lax.rem(me // 2 + mixed, 2)
        x = lax.rem(me // 16 + mixed // 2, 4)
        y = lax.rem((me // 64) * 2 + lax.rem(me, 2) + mixed // 8, 4)
        z = lax.rem(me // 4 + mixed // 32, 4)
        return (y // 2) * 64 + x * 16 + z * 4 + core * 2 + lax.rem(y, 2)

    def scatter(src, dst, first, count, send_sem, recv_sem):
        part = pl.ds(first, count)
        pltpu.make_async_copy(
            src.at[part, :, pl.ds(me, 1)], dst.at[part, :, pl.ds(me, 1)], recv_sem
        ).start()

        def send(step, _):
            peer = peer_at(step)
            pltpu.make_async_remote_copy(
                src_ref=src.at[part, :, pl.ds(peer, 1)],
                dst_ref=dst.at[part, :, pl.ds(me, 1)],
                send_sem=send_sem,
                recv_sem=recv_sem,
                device_id=(peer // 2, lax.rem(peer, 2)),
                device_id_type=MESH,
            ).start()
            return 0

        lax.fori_loop(1, DEV, send, 0)

    def arrived(src, dst, first, count, recv_sem):
        part = pl.ds(first, count)
        pltpu.make_async_copy(src.at[part], dst.at[part], recv_sem).wait()

    def all_sent(src, dst, send_sem):
        part = pl.ds(0, DEV - 1)
        pltpu.make_async_copy(src.at[:, :, part], dst.at[:, :, part], send_sem).wait()

    for load in loads:
        load.wait()

    row = lax.broadcasted_iota(jnp.int32, (128, 128), 0)
    lane = lax.broadcasted_iota(jnp.int32, (128, 128), 1)
    left = lane < 64
    odd_bin = 2 * (row + 256 * lax.rem(lane, 64)) + 1
    angle = (me * odd_bin).astype(F32) * (2.0 * math.pi / (2 * TOTAL // LOCAL))
    own = (jnp.cos(angle), -jnp.sin(angle))
    turn_f[0], turn_f[1] = own
    turn_d[0] = jnp.ones((128, 128), F32)
    turn_d[1] = jnp.zeros((128, 128), F32)
    tw = lambda i: (vecs[2 * i], vecs[2 * i + 1])

    per_f = LOCAL // FWD_CHUNKS

    def forward(g, _):
        for pair in range(0, 8, 2):
            cols = []
            for cs in (pair, pair + 1):
                a = a_ref[g, pl.ds(cs, 64, stride=8), :].astype(F32)
                b = b_ref[g, pl.ds(cs, 64, stride=8), :].astype(F32)
                lo = jnp.where(left[:64], a, pltpu.roll(b, 64, 1))
                hi = jnp.where(left[:64], pltpu.roll(a, 64, 1), b)
                cols.append(jnp.concatenate([lo, hi], 0).astype(BF16))
            x = jnp.concatenate(cols, 1)
            u = dot(mats[0], jnp.concatenate([x, x], 0))
            rows = []
            for i in range(2):
                v = times((u[:128, 128 * i : 128 * i + 128], u[128:, 128 * i : 128 * i + 128]), tw(0))
                rows.append(jnp.concatenate(v, 1))
            vh, vl = halves(jnp.concatenate(rows, 0))
            y = dot(vh, mats[1]) + dot(vl, mats[1]) + dot(vh, mats[2])
            for i in range(2):
                t = (turn_f[0], turn_f[1])
                r = times((y[128 * i : 128 * i + 128, :128], y[128 * i : 128 * i + 128, 128:]), t)
                sent[8 * g + pair + i, 0] = r[0]
                sent[8 * g + pair + i, 1] = r[1]
                turn_f[0], turn_f[1] = times(t, tw(1))

        @pl.when(g == 0)
        def _():
            pl.semaphore_wait(barrier, DEV - 1)

        scatter(sent, got, 8 * g, 8, send_f, recv_f.at[g])
        return 0

    lax.fori_loop(0, FWD_CHUNKS, forward, 0)

    def devices_digit(g, _):
        arrived(sent, got, 8 * g, 8, recv_f.at[g])
        for part in range(0, 8, 4):
            first = 8 * g + part
            x = jnp.concatenate([got[first + i].reshape(256, 128) for i in range(4)], 1)
            xh, xl = halves(x)
            y = dot(mats[3], xh) + dot(mats[3], xl) + dot(mats[4], xh)
            for i in range(4):
                t = (turn_d[0], turn_d[1])
                r = times((y[:128, 128 * i : 128 * i + 128], y[128:, 128 * i : 128 * i + 128]), t)
                mid[first + i, 0] = r[0]
                mid[first + i, 1] = r[1]
                turn_d[0], turn_d[1] = times(t, tw(2))
        return 0

    lax.fori_loop(0, FWD_CHUNKS, devices_digit, 0)

    lane8 = lax.broadcasted_iota(jnp.int32, (8, 128), 1)
    sign = jnp.where(lane8 < 64, 1.0, -1.0).astype(F32)

    def product(t, _):
        rows = pl.ds(pl.multiple_of(8 * t, 8), 8)
        bins = small_dft([(mid[i, 0, rows, :], mid[i, 1, rows, :]) for i in range(LOCAL)], -1)
        prod = []
        for x in bins:
            y = (pltpu.roll(x[0], 64, 1), pltpu.roll(x[1], 64, 1))
            prod.append(times(x, y))
        folded = []
        for i in range(16):
            p, q = prod[i], prod[i + 16]
            f = (p[0] + sign * q[0], p[1] + sign * q[1])
            w = (vecs[14, pl.ds(i, 1), :], vecs[15, pl.ds(i, 1), :])
            folded.append(times(f, w))
        for i, v in enumerate(small_dft(folded, 1)):
            quot[i, 0, rows, :] = v[0]
            quot[i, 1, rows, :] = v[1]
        return 0

    lax.fori_loop(0, 16, product, 0)

    turn_d[0], turn_d[1] = tw(3)
    per_i = 4 // INV_CHUNKS

    def devices_back(chunk, _):
        for part in range(per_i):
            first = 4 * (chunk * per_i + part)
            cols = []
            for i in range(4):
                t = (turn_d[0], turn_d[1])
                r = times((quot[first + i, 0], quot[first + i, 1]), t)
                cols.append(jnp.concatenate(r, 0))
                turn_d[0], turn_d[1] = times(t, tw(4))
            xh, xl = halves(jnp.concatenate(cols, 1))
            y = dot(mats[5], xh) + dot(mats[5], xl) + dot(mats[6], xh)
            for i in range(4):
                back[first + i, 0] = y[:128, 128 * i : 128 * i + 128]
                back[first + i, 1] = y[128:, 128 * i : 128 * i + 128]
        scatter(back, home, 4 * chunk * per_i, 4 * per_i, send_i, recv_i.at[chunk])
        return 0

    lax.fori_loop(0, INV_CHUNKS, devices_back, 0)

    turn_f[0], turn_f[1] = times((own[0], -own[1]), tw(6))

    def inverse(g, _):
        @pl.when(lax.rem(g, per_i) == 0)
        def _():
            arrived(back, home, 4 * g, 4 * per_i, recv_i.at[g // per_i])

        for pair in range(0, 4, 2):
            rows = []
            for i in range(2):
                t = (turn_f[0], turn_f[1])
                at = 4 * g + pair + i
                rows.append(jnp.concatenate(times((home[at, 0], home[at, 1]), t), 1))
                turn_f[0], turn_f[1] = times(t, tw(5))
            xh, xl = halves(jnp.concatenate(rows, 0))
            v = dot(xh, mats[7]) + dot(xl, mats[7]) + dot(xh, mats[8])
            c, s = tw(0)
            cols = []
            for i in range(2):
                vi = times((v[128 * i : 128 * i + 128, :128], v[128 * i : 128 * i + 128, 128:]), (c, -s))
                cols.append(jnp.concatenate(vi, 0))
            vh, vl = halves(jnp.concatenate(cols, 1))
            o = dot(mats[9], vh) + dot(mats[9], vl) + dot(mats[10], vh)
            for i in range(2):
                o0, o1 = o[:128, 128 * i : 128 * i + 128], o[128:, 128 * i : 128 * i + 128]
                cs = 2 * (pair + i)
                out_ref[g, pl.ds(cs, 128, stride=8), :] = jnp.where(left, o0, pltpu.roll(o1, 64, 1))
                out_ref[g, pl.ds(cs + 1, 128, stride=8), :] = jnp.where(left, pltpu.roll(o0, 64, 1), o1)
        pltpu.make_async_copy(out_ref.at[g], out_hbm.at[g], out_sem).start()
        return 0

    lax.fori_loop(0, 4, inverse, 0)
    pltpu.make_async_copy(out_ref, out_hbm, out_sem).wait()
    all_sent(sent, got, send_f)
    all_sent(back, home, send_i)


def on_device(limbs_a, limbs_b):
    def tiles(x):
        return x.reshape(4, 8, 64, 128).transpose(0, 2, 1, 3).reshape(4, 512, 128)

    out = pl.pallas_call(
        kernel,
        out_shape=jax.ShapeDtypeStruct((4, 1024, 128), F32),
        in_specs=[pl.BlockSpec(memory_space=pl.ANY)] * 4,
        out_specs=pl.BlockSpec(memory_space=pl.ANY),
        scratch_shapes=[
            pltpu.VMEM((4, 512, 128), jnp.int32),
            pltpu.VMEM((4, 512, 128), jnp.int32),
            pltpu.VMEM((11, 256, 256), BF16),
            pltpu.VMEM((16, 128, 128), F32),
            pltpu.VMEM((4, 1024, 128), F32),
            pltpu.VMEM((LOCAL, 2, 128, 128), F32),
            pltpu.VMEM((LOCAL, 2, 128, 128), F32),
            pltpu.VMEM((LOCAL, 2, 128, 128), F32),
            pltpu.VMEM((16, 2, 128, 128), F32),
            pltpu.VMEM((16, 2, 128, 128), F32),
            pltpu.VMEM((16, 2, 128, 128), F32),
            pltpu.VMEM((2, 128, 128), F32),
            pltpu.VMEM((2, 128, 128), F32),
            pltpu.SemaphoreType.DMA((4,)),
            pltpu.SemaphoreType.DMA,
            pltpu.SemaphoreType.DMA,
            pltpu.SemaphoreType.DMA((FWD_CHUNKS,)),
            pltpu.SemaphoreType.DMA,
            pltpu.SemaphoreType.DMA((INV_CHUNKS,)),
        ],
        compiler_params=pltpu.CompilerParams(
            collective_id=0, has_side_effects=True, vmem_limit_bytes=52 << 20
        ),
    )(tiles(limbs_a), tiles(limbs_b), jnp.asarray(matrix_tables()), jnp.asarray(vector_tables()))
    return out.reshape(4, 128, 8, 128).transpose(0, 2, 1, 3).reshape(LOCAL, ROWS)


def solution(mesh):
    placed = (P(("fft", "grp"), None), P(("fft", "grp"), None))
    return jax.shard_map(
        on_device, mesh=mesh, in_specs=placed, out_specs=P(("fft", "grp"), None), check_vma=False
    )
```

profile of v0, /device:TPU:1, one launch (start us, length us, event | category | flops | bytes accessed | tf_op | source)
XLA Modules:
  0.0 99.9 jit_solution(2543490640460067532)
XLA Ops:
  0.0 0.0 copy-start
  0.0 1.2 %copy-done = s32[32,8192]{1,0:T(8,128)S(1)} copy-done((s32[32,8192]{1,0:T(8,128)S(1)}, s32[32,8192]{1,0:T(8,128)}, u32[]{:S(2)}) %copy-start) | copy-done | bytes 1048600
  1.2 95.7 %shard_map.46 = f32[4,1024,128]{2,1,0:T(8,128)} custom-call(s32[4,512,128]{2,1,0:T(8,128)S(1)} %bitcast.15, s32[4,512,128]{2,1,0:T(8,128)} %bitcast.17, bf16[11,256,256]{2,1,0:T(8,128)(2,1)} %constant.4.clone.mats_hbm, f32[16,128,128]{2,1,0:T(8,128)} %constant.5.clone.vecs_hbm), custom_call_target="tpu_custom_call" | custom-call | tf_op jit(solution)/shard_map/pallas_call | solution.py:345
  96.9 3.0 %copy.6 = f32[32,16384]{1,0:T(8,128)} copy(f32[32,16384]{1,0:T(8,128)} %bitcast.16) | data formatting | bytes 4194304
Async XLA Ops:
  0.0 1.2 %copy-start = (s32[32,8192]{1,0:T(8,128)S(1)}, s32[32,8192]{1,0:T(8,128)}, u32[]{:S(2)}) copy-start(s32[32,8192]{1,0:T(8,128)} %param.4) | copy-start | bytes 3145732
where the time goes:
time: 100 us; the launch traced here: 99.9 us
  Pallas kernels  95.7 us (96%)
  local copies, waits for them, and re-layouts  4.27 us (4%)
    pallas_call x1, Pallas kernels, on_device(): pl.pallas_call(kernel, out_shape=jax.ShapeDtypeStruct((4, 1024, 128), F32...  95.7 us
    unnamed x3, local copies, waits for them, and re-layouts  4.27 us

commit v1 on v0

v1 whole, which is shorter than its diff:
```python
import functools
import math

import jax
import jax.numpy as jnp
import ml_dtypes
import numpy as np
from jax import lax
from jax.experimental import pallas as pl
from jax.experimental.pallas import tpu as pltpu
from jax.sharding import PartitionSpec as P

MESH = pl.DeviceIdType.MESH
ROWS = 16384
COLS = 4096
TOTAL = ROWS * COLS
DIGIT_VAR = 5461.25
DEV = 128
LOCAL = COLS // DEV
HALVES = 2
PAIRS = LOCAL // 2
FWD_CHUNKS = 4
INV_CHUNKS = 2
F32 = jnp.float32
BF16 = jnp.bfloat16


def turn(num, den):
    angle = (np.asarray(num, np.int64) % den) * (2.0 * math.pi / den)
    return np.cos(angle), np.sin(angle)


def split_pair(table):
    high = table.astype(ml_dtypes.bfloat16)
    low = (table - high.astype(np.float64)).astype(ml_dtypes.bfloat16)
    return high, low


@functools.lru_cache(None)
def matrix_tables():
    ka = np.arange(128)
    lane = np.arange(64)
    order = np.concatenate([2 * np.arange(64), 2 * np.arange(64) + 1])
    c, s = turn(np.outer(2 * ka + 1, order), 512)
    first = split_pair(np.concatenate([c, -s], 0))
    first = np.concatenate([first[0], first[1]], 1)
    c, s = turn(np.outer(lane, lane), 64)
    z = np.zeros_like(c)
    c2, s2 = np.block([[c, z], [z, c]]), np.block([[s, z], [z, s]])
    lanes_inv = split_pair(np.block([[c2, s2], [-s2, c2]]))
    at = np.arange(128)
    at = at // 64 * 32 + at % 64 // 32 * 64 + at % 32
    c2, s2 = c2[:, at], s2[:, at]
    lanes_fwd = split_pair(np.block([[c2, -s2], [s2, c2]]))
    c, s = turn(np.outer(ka, ka), 128)
    dev_fwd = split_pair(np.block([[c, s], [-s, c]]))
    dev_inv = split_pair(np.block([[c, -s], [s, c]]))
    scale = 2.0 / (TOTAL * DIGIT_VAR * math.sqrt(TOTAL // 2))
    order = np.concatenate([2 * np.arange(128), 2 * np.arange(128) + 1])
    c, s = turn(np.outer(order, 2 * ka + 1), 512)
    last = split_pair(np.concatenate([c, -s], 1) * scale)
    mats = [first, *lanes_fwd, *dev_fwd, *dev_inv, *lanes_inv, *last]
    return np.stack(mats)


@functools.lru_cache(None)
def vector_tables():
    ka = np.arange(128)[:, None]
    lane = np.arange(128)[None, :]
    low, par = lane % 64, lane // 64
    two = par + 2 * (lane % 64 // 32)
    zero = 0 * lane
    k1 = ka + 256 * low
    k1_sent = ka + 256 * (32 * par + lane % 32)
    pairs = [
        turn(-low * (2 * ka + 1), 2 * ROWS),
        turn(-(2 * k1_sent + 1), 2 * TOTAL),
        turn(-ka * par, COLS),
        turn(-2 * ka + zero, COLS),
        turn(ka * two, COLS),
        turn(4 * ka + zero, COLS),
        turn(2 * (2 * k1 + 1), 2 * TOTAL),
        turn(par * (2 * k1 + 1), 2 * TOTAL),
        turn(-ka * par, 32),
        turn(ka * two, 32),
    ]
    return np.stack([t for pair in pairs for t in pair]).astype(np.float32)


def times(a, b):
    return a[0] * b[0] - a[1] * b[1], a[0] * b[1] + a[1] * b[0]


def turned(value, num, den):
    num %= den
    re, im = value
    if num == 0:
        return value
    if 4 * num == den:
        return -im, re
    if 2 * num == den:
        return -re, -im
    if 4 * num == 3 * den:
        return im, -re
    c, s = math.cos(2 * math.pi * num / den), math.sin(2 * math.pi * num / den)
    if 8 * num % den == 0:
        root = math.sqrt(0.5)
        sc, ss = math.copysign(1.0, c), math.copysign(1.0, s)
        first = re if sc > 0 else -re
        first = first - im if ss > 0 else first + im
        second = re if ss > 0 else -re
        second = second + im if sc > 0 else second - im
        return first * root, second * root
    return re * c - im * s, re * s + im * c


def small_dft(values, sign):
    n = len(values)
    if n == 1:
        return values
    half = n // 2
    even = [(a[0] + b[0], a[1] + b[1]) for a, b in zip(values[:half], values[half:])]
    odd = [
        turned((a[0] - b[0], a[1] - b[1]), sign * i, n)
        for i, (a, b) in enumerate(zip(values[:half], values[half:]))
    ]
    even, odd = small_dft(even, sign), small_dft(odd, sign)
    return [v for pair in zip(even, odd) for v in pair]


def halves(value):
    high = value.astype(BF16)
    return high, (value - high.astype(F32)).astype(BF16)


def dot(a, b):
    return jnp.dot(a, b, preferred_element_type=F32)


def kernel(
    a_hbm, b_hbm, mats_hbm, vecs_hbm, out_ref,
    a_ref, b_ref, mats, vecs, sent, got, mid, quot, back, home, turn_f, turn_d,
    in_sem, ready, send_f, recv_f, send_i, recv_i,
):
    fft, grp = lax.axis_index("fft"), lax.axis_index("grp")
    me = fft * 2 + grp
    barrier = pltpu.get_barrier_semaphore()

    loads = [
        pltpu.make_async_copy(src, dst, in_sem.at[i])
        for i, (src, dst) in enumerate(
            ((vecs_hbm, vecs), (a_hbm, a_ref), (b_hbm, b_ref), (mats_hbm, mats))
        )
    ]
    for load in loads:
        load.start()

    high, low = lax.div(me, 16), lax.rem(me, 16)

    def signal(sem, peer):
        pl.semaphore_signal(
            sem, inc=1, device_id=(lax.div(peer, 2), lax.rem(peer, 2)), device_id_type=MESH
        )

    for step in range(1, 16):
        signal(barrier, high * 16 + lax.rem(low + step, 16))
    across = [lax.rem(high + step, 8) * 16 + low for step in range(1, 8)]
    for peer in across:
        signal(barrier, peer)

    core, z, x = lax.rem(fft, 2), lax.rem(lax.div(fft, 2), 4), lax.rem(lax.div(fft, 8), 4)
    y = lax.div(fft, 32) * 2 + grp
    z_core = [
        lax.rem(z + j % 4, 4) * 2 + (core if j < 4 else 1 - core) for j in range(8)
    ]

    def each_peer(visit):
        def eight(dx, dy, first):
            xs = [lax.rem(x + (dx + t), 4) * 8 for t in range(4)]
            ys = [lax.rem(y + (dy + t), 4) for t in range(4)]
            highs = [lax.div(v, 2) * 32 for v in ys]
            lows = [lax.rem(v, 2) for v in ys]
            for j in range(first, 8):
                t = (2 * j + j // 2) % 4
                visit(z_core[j] + xs[(j + j // 4) % 4] + highs[t], lows[t])

        eight(0, 0, 1)

        def some(i, _):
            eight(lax.div(i, 4), lax.rem(i, 4), 0)
            return 0

        lax.fori_loop(1, 16, some, 0)

    def scatter(src, dst, first, count, send_sem, recv_sem):
        part = pl.ds(first, count)
        own = pl.ds(me, 1)
        pltpu.make_async_copy(src.at[part, :, own], dst.at[part, :, own], recv_sem).start()

        def send(peer_fft, peer_grp):
            pltpu.make_async_remote_copy(
                src_ref=src.at[part, :, pl.ds(peer_fft * 2 + peer_grp, 1)],
                dst_ref=dst.at[part, :, own],
                send_sem=send_sem,
                recv_sem=recv_sem,
                device_id=(peer_fft, peer_grp),
                device_id_type=MESH,
            ).start()

        each_peer(send)

    def arrived(src, dst, first, count, recv_sem):
        part = pl.ds(first, count)
        pltpu.make_async_copy(src.at[part], dst.at[part], recv_sem).wait()

    def all_sent(src, dst, send_sem):
        part = pl.ds(0, DEV - 1)
        pltpu.make_async_copy(src.at[:, :, part], dst.at[:, :, part], send_sem).wait()

    row = lax.broadcasted_iota(jnp.int32, (128, 128), 0)
    lane = lax.broadcasted_iota(jnp.int32, (128, 128), 1)
    left = lane < 64
    low32 = lax.rem(lane, 64) < 32
    tw = lambda i: (vecs[2 * i], vecs[2 * i + 1])

    def own_turn(kb):
        angle = (me * (2 * (row + 256 * kb) + 1)).astype(F32)
        angle = angle * (2.0 * math.pi / (2 * TOTAL // LOCAL))
        return jnp.cos(angle), jnp.sin(angle)

    c, s = own_turn(32 * lax.div(lane, 64) + lax.rem(lane, 32))
    turn_f[0], turn_f[1] = c, -s
    for load in loads:
        load.wait()
    pl.semaphore_wait(barrier, 22)
    for peer in across:
        signal(ready, peer)

    def forward(g, _):
        for pair in range(0, 8, 2):
            cols = []
            for cs in (pair, pair + 1):
                a = a_ref[g, pl.ds(cs, 64, stride=8), :].astype(F32)
                b = b_ref[g, pl.ds(cs, 64, stride=8), :].astype(F32)
                lo = jnp.where(left[:64], a, pltpu.roll(b, 64, 1))
                hi = jnp.where(left[:64], pltpu.roll(a, 64, 1), b)
                cols.append(jnp.concatenate([lo, hi], 0).astype(BF16))
            u_in = jnp.concatenate(cols, 1)
            u = dot(mats[0], jnp.concatenate([u_in, u_in], 0))
            rows = []
            for i in range(2):
                v = times((u[:128, 128 * i : 128 * i + 128], u[128:, 128 * i : 128 * i + 128]), tw(0))
                rows.append(jnp.concatenate(v, 1))
            vh, vl = halves(jnp.concatenate(rows, 0))
            f = dot(vh, mats[1]) + dot(vl, mats[1]) + dot(vh, mats[2])
            r = []
            for i in range(2):
                t = (turn_f[0], turn_f[1])
                r.append(times((f[128 * i : 128 * i + 128, :128], f[128 * i : 128 * i + 128, 128:]), t))
                turn_f[0], turn_f[1] = times(t, tw(1))
            at = 4 * g + pair // 2
            for i in range(2):
                sent[at, i] = jnp.where(left, r[0][i], pltpu.roll(r[1][i], 64, 1))
                sent[PAIRS + at, i] = jnp.where(left, pltpu.roll(r[0][i], 64, 1), r[1][i])

        @pl.when(g == 0)
        def _():
            pl.semaphore_wait(ready, 7)

        scatter(sent, got, 4 * g, 4, send_f, recv_f.at[g])
        return 0

    lax.fori_loop(0, 4, forward, 0)

    def second(g, _):
        scatter(sent, got, PAIRS + 4 * g, 4, send_f, recv_f.at[4 + g])
        return 0

    lax.fori_loop(0, 4, second, 0)

    lane8 = lax.broadcasted_iota(jnp.int32, (8, 128), 1)
    left8 = lane8 < 64
    low8 = lax.rem(lane8, 64) < 32
    sign1 = jnp.where(left8, 1.0, -1.0).astype(F32)
    sign2 = jnp.where(low8, 1.0, -1.0).astype(F32)

    def columns(h, _):
        turn_d[0], turn_d[1] = tw(2)

        def devices_digit(g, _):
            first = PAIRS * h + 4 * g
            arrived(sent, got, first, 4, recv_f.at[4 * h + g])
            x_in = jnp.concatenate([got[first + i].reshape(256, 128) for i in range(4)], 1)
            xh, xl = halves(x_in)
            f = dot(mats[3], xh) + dot(mats[3], xl) + dot(mats[4], xh)
            for i in range(4):
                t = (turn_d[0], turn_d[1])
                r = times((f[:128, 128 * i : 128 * i + 128], f[128:, 128 * i : 128 * i + 128]), t)
                mid[4 * g + i, 0] = r[0]
                mid[4 * g + i, 1] = r[1]
                turn_d[0], turn_d[1] = times(t, tw(3))
            return 0

        lax.fori_loop(0, 4, devices_digit, 0)

        def product(t, _):
            rows = pl.ds(pl.multiple_of(8 * t, 8), 8)
            bins = small_dft([(mid[i, 0, rows, :], mid[i, 1, rows, :]) for i in range(PAIRS)], -1)
            folded = []
            for i, v in enumerate(bins):
                w = (vecs[16, pl.ds(i, 1), :], vecs[17, pl.ds(i, 1), :])
                v = times(v, w)
                v = tuple(pltpu.roll(e, 64, 1) + sign1 * e for e in v)
                o = tuple(jnp.where(low8, pltpu.roll(e, 96, 1), pltpu.roll(e, 32, 1)) for e in v)
                p = times(v, o)
                folded.append(tuple(pltpu.roll(e, 64, 1) + sign1 * e for e in p))
            packed = []
            for i in range(8):
                p, q = folded[i], folded[i + 8]
                q = (jnp.where(left8, q[0], -q[1]), jnp.where(left8, q[1], q[0]))
                w = (vecs[18, pl.ds(i, 1), :], vecs[19, pl.ds(i, 1), :])
                packed.append(times((p[0] + sign2 * q[0], p[1] + sign2 * q[1]), w))
            for i, v in enumerate(small_dft(packed, 1)):
                quot[i, 0, rows, :] = v[0]
                quot[i, 1, rows, :] = v[1]
            return 0

        lax.fori_loop(0, 16, product, 0)

        turn_d[0], turn_d[1] = tw(4)

        def devices_back(g, _):
            cols = []
            for i in range(4):
                t = (turn_d[0], turn_d[1])
                r = times((quot[4 * g + i, 0], quot[4 * g + i, 1]), t)
                cols.append(jnp.concatenate(r, 0))
                turn_d[0], turn_d[1] = times(t, tw(5))
            xh, xl = halves(jnp.concatenate(cols, 1))
            f = dot(mats[5], xh) + dot(mats[5], xl) + dot(mats[6], xh)
            first = 8 * h + 4 * g
            for i in range(4):
                back[first + i, 0] = f[:128, 128 * i : 128 * i + 128]
                back[first + i, 1] = f[128:, 128 * i : 128 * i + 128]
            scatter(back, home, first, 4, send_i, recv_i.at[2 * h + g])
            return 0

        lax.fori_loop(0, 2, devices_back, 0)
        return 0

    lax.fori_loop(0, HALVES, columns, 0)

    turn_f[0], turn_f[1] = times(own_turn(lax.rem(lane, 64)), tw(7))

    def inverse(g, _):
        @pl.when(lax.rem(g, 2) == 0)
        def _():
            arrived(back, home, 2 * g, 4, recv_i.at[lax.div(g, 2)])
            arrived(back, home, 8 + 2 * g, 4, recv_i.at[2 + lax.div(g, 2)])

        for pair in range(2):
            at = 2 * g + pair
            both = ([], [])
            for i in range(2):
                p, q = home[at, i], home[8 + at, i]
                both[0].append(jnp.where(low32, p, pltpu.roll(q, 32, 1)))
                both[1].append(jnp.where(low32, pltpu.roll(p, 96, 1), q))
            rows = []
            for v in both:
                t = (turn_f[0], turn_f[1])
                rows.append(jnp.concatenate(times(v, t), 1))
                turn_f[0], turn_f[1] = times(t, tw(6))
            xh, xl = halves(jnp.concatenate(rows, 0))
            v = dot(xh, mats[7]) + dot(xl, mats[7]) + dot(xh, mats[8])
            c, s = tw(0)
            cols = []
            for i in range(2):
                vi = times((v[128 * i : 128 * i + 128, :128], v[128 * i : 128 * i + 128, 128:]), (c, -s))
                cols.append(jnp.concatenate(vi, 0))
            vh, vl = halves(jnp.concatenate(cols, 1))
            o = dot(mats[9], vh) + dot(mats[9], vl) + dot(mats[10], vh)
            for i in range(2):
                o0, o1 = o[:128, 128 * i : 128 * i + 128], o[128:, 128 * i : 128 * i + 128]
                cs = 4 * pair + 2 * i
                out_ref[g, pl.ds(cs, 128, stride=8), :] = jnp.where(left, o0, pltpu.roll(o1, 64, 1))
                out_ref[g, pl.ds(cs + 1, 128, stride=8), :] = jnp.where(left, pltpu.roll(o0, 64, 1), o1)
        return 0

    lax.fori_loop(0, 4, inverse, 0)
    all_sent(sent, got, send_f)
    all_sent(back, home, send_i)


def on_device(limbs_a, limbs_b):
    def tiles(x):
        return x.reshape(4, 8, 64, 128).transpose(0, 2, 1, 3).reshape(4, 512, 128)

    out = pl.pallas_call(
        kernel,
        out_shape=pltpu.VMEM((4, 1024, 128), F32),
        in_specs=[pl.BlockSpec(memory_space=pltpu.HBM)] * 4,
        out_specs=pl.BlockSpec(memory_space=pltpu.VMEM),
        scratch_shapes=[
            pltpu.VMEM((4, 512, 128), jnp.int32),
            pltpu.VMEM((4, 512, 128), jnp.int32),
            pltpu.VMEM((11, 256, 256), BF16),
            pltpu.VMEM((20, 128, 128), F32),
            pltpu.VMEM((LOCAL, 2, 128, 128), F32),
            pltpu.VMEM((LOCAL, 2, 128, 128), F32),
            pltpu.VMEM((PAIRS, 2, 128, 128), F32),
            pltpu.VMEM((8, 2, 128, 128), F32),
            pltpu.VMEM((16, 2, 128, 128), F32),
            pltpu.VMEM((16, 2, 128, 128), F32),
            pltpu.VMEM((2, 128, 128), F32),
            pltpu.VMEM((2, 128, 128), F32),
            pltpu.SemaphoreType.DMA((4,)),
            pltpu.SemaphoreType.REGULAR,
            pltpu.SemaphoreType.DMA,
            pltpu.SemaphoreType.DMA((8,)),
            pltpu.SemaphoreType.DMA,
            pltpu.SemaphoreType.DMA((4,)),
        ],
        compiler_params=pltpu.CompilerParams(
            collective_id=0, has_side_effects=True, vmem_limit_bytes=60 << 20
        ),
    )(tiles(limbs_a), tiles(limbs_b), jnp.asarray(matrix_tables()), jnp.asarray(vector_tables()))
    return out.reshape(4, 128, 8, 128).transpose(0, 2, 1, 3).reshape(LOCAL, ROWS)


def solution(mesh):
    placed = (P(("fft", "grp"), None), P(("fft", "grp"), None))
    return jax.shard_map(
        on_device, mesh=mesh, in_specs=placed, out_specs=P(("fft", "grp"), None), check_vma=False
    )
```

time: 100 us -> 88.9 us (0.89)
  Pallas kernels: 95.7 us -> 87.5 us
  local copies, waits for them, and re-layouts: 4.27 us -> 1.32 us
    pallas_call x1, Pallas kernels: 95.7 us -> 87.5 us  [on_device(): pl.pallas_call(kernel, out_shape=pltpu.VMEM((4, 1024, 128), F32), in_spec...]
    unnamed x3 -> x1, local copies, waits for them, and re-layouts: 4.27 us -> 1.32 us
where the time goes in v1:
time: 88.9 us; the launch traced here: 88.8 us
  Pallas kernels  87.5 us (98%)
  local copies, waits for them, and re-layouts  1.32 us (1%)
    pallas_call x1, Pallas kernels, on_device(): pl.pallas_call(kernel, out_shape=pltpu.VMEM((4, 1024, 128), F32), in_spec...  87.5 us

profile of v1, /device:TPU:1, one launch (start us, length us, event | category | flops | bytes accessed | tf_op | source)
XLA Modules:
  0.0 88.8 jit_solution(17110084610047159752)
XLA Ops:
  0.0 87.5 %shard_map.46 = f32[4,1024,128]{2,1,0:T(8,128)S(1)} custom-call(s32[4,512,128]{2,1,0:T(8,128)} %bitcast.16, s32[4,512,128]{2,1,0:T(8,128)} %bitcast.17, bf16[11,256,256]{2,1,0:T(8,128)(2,1)} %constant.4.clone.mats_hbm, f32[20,128,128]{2,1,0:T(8,128)} %constant.5.clone.vecs_hbm), custom_call_target="tpu_custom_call" | custom-call | tf_op jit(solution)/shard_map/pallas_call | solution.py:398
  87.5 1.3 %copy.6 = f32[32,16384]{1,0:T(8,128)} copy(f32[32,16384]{1,0:T(8,128)S(1)} %bitcast.15) | data formatting | bytes 4194304

commit v2 on v1

--- a/solution.py
+++ b/solution.py
@@ -146,11 +146,11 @@
     me = fft * 2 + grp
     barrier = pltpu.get_barrier_semaphore()
 
+    parts = [(a_hbm, a_ref, 0, 1), (b_hbm, b_ref, 0, 1), (mats_hbm, mats, 0, 3), (vecs_hbm, vecs, 0, 4)]
+    parts += [(a_hbm, a_ref, 1, 3), (b_hbm, b_ref, 1, 3), (mats_hbm, mats, 3, 8), (vecs_hbm, vecs, 4, 16)]
     loads = [
-        pltpu.make_async_copy(src, dst, in_sem.at[i])
-        for i, (src, dst) in enumerate(
-            ((vecs_hbm, vecs), (a_hbm, a_ref), (b_hbm, b_ref), (mats_hbm, mats))
-        )
+        pltpu.make_async_copy(src.at[pl.ds(at, n)], dst.at[pl.ds(at, n)], in_sem.at[i])
+        for i, (src, dst, at, n) in enumerate(parts)
     ]
     for load in loads:
         load.start()
@@ -230,14 +230,11 @@
 
     c, s = own_turn(32 * lax.div(lane, 64) + lax.rem(lane, 32))
     turn_f[0], turn_f[1] = c, -s
-    for load in loads:
+    for load in loads[:4]:
         load.wait()
-    pl.semaphore_wait(barrier, 22)
-    for peer in across:
-        signal(ready, peer)
-
-    def forward(g, _):
-        for pair in range(0, 8, 2):
+
+    def rows_forward(g, first, last):
+        for pair in range(first, last, 2):
             cols = []
             for cs in (pair, pair + 1):
                 a = a_ref[g, pl.ds(cs, 64, stride=8), :].astype(F32)
@@ -263,14 +260,49 @@
                 sent[at, i] = jnp.where(left, r[0][i], pltpu.roll(r[1][i], 64, 1))
                 sent[PAIRS + at, i] = jnp.where(left, pltpu.roll(r[0][i], 64, 1), r[1][i])
 
-        @pl.when(g == 0)
-        def _():
-            pl.semaphore_wait(ready, 7)
-
+    def forward(g, _):
+        rows_forward(g, 0, 8)
         scatter(sent, got, 4 * g, 4, send_f, recv_f.at[g])
         return 0
 
-    lax.fori_loop(0, 4, forward, 0)
+    rows_forward(0, 0, 4)
+    pl.semaphore_wait(barrier, 22)
+    for step, peer in enumerate(across):
+        signal(ready.at[step], peer)
+    first_part, own = pl.ds(0, 2), pl.ds(me, 1)
+    pltpu.make_async_copy(sent.at[first_part, :, own], got.at[first_part, :, own], recv_f.at[8]).start()
+
+    def first_send(peer):
+        pltpu.make_async_remote_copy(
+            src_ref=sent.at[first_part, :, pl.ds(peer, 1)],
+            dst_ref=got.at[first_part, :, own],
+            send_sem=send_f,
+            recv_sem=recv_f.at[8],
+            device_id=(lax.div(peer, 2), lax.rem(peer, 2)),
+            device_id_type=MESH,
+        ).start()
+
+    for step in range(1, 16):
+        first_send(high * 16 + lax.rem(low + step, 16))
+
+    def first_sends(step, _):
+        pl.semaphore_wait(ready.at[step - 1], 1)
+        base = lax.rem(high + 8 - step, 8) * 16
+
+        def some(i, _):
+            for j in range(4):
+                first_send(base + lax.rem(low + 4 * i + j, 16))
+            return 0
+
+        lax.fori_loop(0, 4, some, 0)
+        return 0
+
+    lax.fori_loop(1, 8, first_sends, 0)
+    for load in loads[4:]:
+        load.wait()
+    rows_forward(0, 4, 8)
+    scatter(sent, got, 2, 2, send_f, recv_f.at[0])
+    lax.fori_loop(1, 4, forward, 0)
 
     def second(g, _):
         scatter(sent, got, PAIRS + 4 * g, 4, send_f, recv_f.at[4 + g])
@@ -289,7 +321,17 @@
 
         def devices_digit(g, _):
             first = PAIRS * h + 4 * g
-            arrived(sent, got, first, 4, recv_f.at[4 * h + g])
+            start = jnp.logical_and(h == 0, g == 0)
+
+            @pl.when(start)
+            def _():
+                arrived(sent, got, 0, 2, recv_f.at[8])
+                arrived(sent, got, 2, 2, recv_f.at[0])
+
+            @pl.when(jnp.logical_not(start))
+            def _():
+                arrived(sent, got, first, 4, recv_f.at[4 * h + g])
+
             x_in = jnp.concatenate([got[first + i].reshape(256, 128) for i in range(4)], 1)
             xh, xl = halves(x_in)
             f = dot(mats[3], xh) + dot(mats[3], xl) + dot(mats[4], xh)
@@ -342,7 +384,8 @@
             for i in range(4):
                 back[first + i, 0] = f[:128, 128 * i : 128 * i + 128]
                 back[first + i, 1] = f[128:, 128 * i : 128 * i + 128]
-            scatter(back, home, first, 4, send_i, recv_i.at[2 * h + g])
+            scatter(back, home, first, 2, send_i, recv_i.at[4 * h + 2 * g])
+            scatter(back, home, first + 2, 2, send_i, recv_i.at[4 * h + 2 * g + 1])
             return 0
 
         lax.fori_loop(0, 2, devices_back, 0)
@@ -353,10 +396,8 @@
     turn_f[0], turn_f[1] = times(own_turn(lax.rem(lane, 64)), tw(7))
 
     def inverse(g, _):
-        @pl.when(lax.rem(g, 2) == 0)
-        def _():
-            arrived(back, home, 2 * g, 4, recv_i.at[lax.div(g, 2)])
-            arrived(back, home, 8 + 2 * g, 4, recv_i.at[2 + lax.div(g, 2)])
+        arrived(back, home, 2 * g, 2, recv_i.at[g])
+        arrived(back, home, 8 + 2 * g, 2, recv_i.at[4 + g])
 
         for pair in range(2):
             at = 2 * g + pair
@@ -413,12 +454,12 @@
             pltpu.VMEM((16, 2, 128, 128), F32),
             pltpu.VMEM((2, 128, 128), F32),
             pltpu.VMEM((2, 128, 128), F32),
-            pltpu.SemaphoreType.DMA((4,)),
-            pltpu.SemaphoreType.REGULAR,
+            pltpu.SemaphoreType.DMA((8,)),
+            pltpu.SemaphoreType.REGULAR((7,)),
+            pltpu.SemaphoreType.DMA,
+            pltpu.SemaphoreType.DMA((9,)),
             pltpu.SemaphoreType.DMA,
             pltpu.SemaphoreType.DMA((8,)),
-            pltpu.SemaphoreType.DMA,
-            pltpu.SemaphoreType.DMA((4,)),
         ],
         compiler_params=pltpu.CompilerParams(
             collective_id=0, has_side_effects=True, vmem_limit_bytes=60 << 20

time: 88.9 us -> 87.3 us (0.982)
  Pallas kernels: 87.5 us -> 85.8 us
    pallas_call x1, Pallas kernels: 87.5 us -> 85.8 us  [on_device(): pl.pallas_call(kernel, out_shape=pltpu.VMEM((4, 1024, 128), F32), in_spec...]
where the time goes in v2:
time: 87.3 us; the launch traced here: 87.1 us
  Pallas kernels  85.8 us (98%)
  local copies, waits for them, and re-layouts  1.32 us (2%)
    pallas_call x1, Pallas kernels, on_device(): pl.pallas_call(kernel, out_shape=pltpu.VMEM((4, 1024, 128), F32), in_spec...  85.8 us

profile of v2, /device:TPU:1, one launch (start us, length us, event | category | flops | bytes accessed | tf_op | source)
XLA Modules:
  0.0 87.1 jit_solution(18260595428937474802)
XLA Ops:
  0.0 85.8 %shard_map.46 = f32[4,1024,128]{2,1,0:T(8,128)S(1)} custom-call(s32[4,512,128]{2,1,0:T(8,128)} %bitcast.16, s32[4,512,128]{2,1,0:T(8,128)} %bitcast.17, bf16[11,256,256]{2,1,0:T(8,128)(2,1)} %constant.4.clone.mats_hbm, f32[20,128,128]{2,1,0:T(8,128)} %constant.5.clone.vecs_hbm), custom_call_target="tpu_custom_call" | custom-call | tf_op jit(solution)/shard_map/pallas_call | solution.py:439
  85.8 1.3 %copy.6 = f32[32,16384]{1,0:T(8,128)} copy(f32[32,16384]{1,0:T(8,128)S(1)} %bitcast.15) | data formatting | bytes 4194304

commit v3 on v2

--- a/solution.py
+++ b/solution.py
@@ -87,6 +87,22 @@
     return np.stack([t for pair in pairs for t in pair]).astype(np.float32)
 
 
+def all_displacements():
+    out = []
+    for i in range(16):
+        for j in range(8):
+            dx, dy = i // 4 + j + j // 4, i % 4 + 2 * j + j // 2
+            out.append((dx % 4, dy % 4, j % 4, j // 4))
+    return out[1:]
+
+
+PEERS = all_displacements()
+
+
+def hops(place):
+    return sum(min(v, 4 - v) for v in place[:3])
+
+
 def times(a, b):
     return a[0] * b[0] - a[1] * b[1], a[0] * b[1] + a[1] * b[0]
 
@@ -140,7 +156,7 @@
 def kernel(
     a_hbm, b_hbm, mats_hbm, vecs_hbm, out_ref,
     a_ref, b_ref, mats, vecs, sent, got, mid, quot, back, home, turn_f, turn_d,
-    in_sem, ready, send_f, recv_f, send_i, recv_i,
+    in_sem, send_f, recv_f, send_i, recv_i,
 ):
     fft, grp = lax.axis_index("fft"), lax.axis_index("grp")
     me = fft * 2 + grp
@@ -155,59 +171,42 @@
     for load in loads:
         load.start()
 
-    high, low = lax.div(me, 16), lax.rem(me, 16)
-
-    def signal(sem, peer):
-        pl.semaphore_signal(
-            sem, inc=1, device_id=(lax.div(peer, 2), lax.rem(peer, 2)), device_id_type=MESH
-        )
-
-    for step in range(1, 16):
-        signal(barrier, high * 16 + lax.rem(low + step, 16))
-    across = [lax.rem(high + step, 8) * 16 + low for step in range(1, 8)]
-    for peer in across:
-        signal(barrier, peer)
-
     core, z, x = lax.rem(fft, 2), lax.rem(lax.div(fft, 2), 4), lax.rem(lax.div(fft, 8), 4)
     y = lax.div(fft, 32) * 2 + grp
-    z_core = [
-        lax.rem(z + j % 4, 4) * 2 + (core if j < 4 else 1 - core) for j in range(8)
-    ]
-
-    def each_peer(visit):
-        def eight(dx, dy, first):
-            xs = [lax.rem(x + (dx + t), 4) * 8 for t in range(4)]
-            ys = [lax.rem(y + (dy + t), 4) for t in range(4)]
-            highs = [lax.div(v, 2) * 32 for v in ys]
-            lows = [lax.rem(v, 2) for v in ys]
-            for j in range(first, 8):
-                t = (2 * j + j // 2) % 4
-                visit(z_core[j] + xs[(j + j // 4) % 4] + highs[t], lows[t])
-
-        eight(0, 0, 1)
-
-        def some(i, _):
-            eight(lax.div(i, 4), lax.rem(i, 4), 0)
-            return 0
-
-        lax.fori_loop(1, 16, some, 0)
+    cores = [core, 1 - core]
+    zs = [lax.rem(z + t, 4) * 2 for t in range(4)]
+    xs = [lax.rem(x + t, 4) * 8 for t in range(4)]
+    ys = [lax.rem(y + t, 4) for t in range(4)]
+    highs = [lax.div(v, 2) * 32 for v in ys]
+    lows = [lax.rem(v, 2) for v in ys]
+
+    def peer_at(dx, dy, dz, dc):
+        return highs[dy] + xs[dx] + zs[dz] + cores[dc], lows[dy]
+
+    def signal(sem, place):
+        pl.semaphore_signal(sem, inc=1, device_id=peer_at(*place), device_id_type=MESH)
+
+    for place in sorted(PEERS, key=lambda d: -hops(d)):
+        signal(barrier, place)
+
+    def send(src, dst, part, place, send_sem, recv_sem):
+        peer = peer_at(*place)
+        pltpu.make_async_remote_copy(
+            src_ref=src.at[part, :, pl.ds(peer[0] * 2 + peer[1], 1)],
+            dst_ref=dst.at[part, :, pl.ds(me, 1)],
+            send_sem=send_sem,
+            recv_sem=recv_sem,
+            device_id=peer,
+            device_id_type=MESH,
+        ).start()
 
     def scatter(src, dst, first, count, send_sem, recv_sem):
         part = pl.ds(first, count)
         own = pl.ds(me, 1)
         pltpu.make_async_copy(src.at[part, :, own], dst.at[part, :, own], recv_sem).start()
 
-        def send(peer_fft, peer_grp):
-            pltpu.make_async_remote_copy(
-                src_ref=src.at[part, :, pl.ds(peer_fft * 2 + peer_grp, 1)],
-                dst_ref=dst.at[part, :, own],
-                send_sem=send_sem,
-                recv_sem=recv_sem,
-                device_id=(peer_fft, peer_grp),
-                device_id_type=MESH,
-            ).start()
-
-        each_peer(send)
+        for place in PEERS:
+            send(src, dst, part, place, send_sem, recv_sem)
 
     def arrived(src, dst, first, count, recv_sem):
         part = pl.ds(first, count)
@@ -266,49 +265,15 @@
         return 0
 
     rows_forward(0, 0, 4)
-    pl.semaphore_wait(barrier, 22)
-    for step, peer in enumerate(across):
-        signal(ready.at[step], peer)
-    first_part, own = pl.ds(0, 2), pl.ds(me, 1)
-    pltpu.make_async_copy(sent.at[first_part, :, own], got.at[first_part, :, own], recv_f.at[8]).start()
-
-    def first_send(peer):
-        pltpu.make_async_remote_copy(
-            src_ref=sent.at[first_part, :, pl.ds(peer, 1)],
-            dst_ref=got.at[first_part, :, own],
-            send_sem=send_f,
-            recv_sem=recv_f.at[8],
-            device_id=(lax.div(peer, 2), lax.rem(peer, 2)),
-            device_id_type=MESH,
-        ).start()
-
-    for step in range(1, 16):
-        first_send(high * 16 + lax.rem(low + step, 16))
-
-    def first_sends(step, _):
-        pl.semaphore_wait(ready.at[step - 1], 1)
-        base = lax.rem(high + 8 - step, 8) * 16
-
-        def some(i, _):
-            for j in range(4):
-                first_send(base + lax.rem(low + 4 * i + j, 16))
-            return 0
-
-        lax.fori_loop(0, 4, some, 0)
-        return 0
-
-    lax.fori_loop(1, 8, first_sends, 0)
+    pl.semaphore_wait(barrier, DEV - 1)
+    scatter(sent, got, 0, 2, send_f, recv_f.at[8])
     for load in loads[4:]:
         load.wait()
     rows_forward(0, 4, 8)
     scatter(sent, got, 2, 2, send_f, recv_f.at[0])
     lax.fori_loop(1, 4, forward, 0)
 
-    def second(g, _):
-        scatter(sent, got, PAIRS + 4 * g, 4, send_f, recv_f.at[4 + g])
-        return 0
-
-    lax.fori_loop(0, 4, second, 0)
+    scatter(sent, got, PAIRS, 4, send_f, recv_f.at[4])
 
     lane8 = lax.broadcasted_iota(jnp.int32, (8, 128), 1)
     left8 = lane8 < 64
@@ -341,6 +306,11 @@
                 mid[4 * g + i, 0] = r[0]
                 mid[4 * g + i, 1] = r[1]
                 turn_d[0], turn_d[1] = times(t, tw(3))
+
+            @pl.when(jnp.logical_and(h == 0, g < 3))
+            def _():
+                scatter(sent, got, PAIRS + 4 * (g + 1), 4, send_f, recv_f.at[5 + g])
+
             return 0
 
         lax.fori_loop(0, 4, devices_digit, 0)
@@ -455,7 +425,6 @@
             pltpu.VMEM((2, 128, 128), F32),
             pltpu.VMEM((2, 128, 128), F32),
             pltpu.SemaphoreType.DMA((8,)),
-            pltpu.SemaphoreType.REGULAR((7,)),
             pltpu.SemaphoreType.DMA,
             pltpu.SemaphoreType.DMA((9,)),
             pltpu.SemaphoreType.DMA,

time: 87.3 us -> 86.3 us (0.989)
  Pallas kernels: 85.8 us -> 84.8 us
    pallas_call x1, Pallas kernels: 85.8 us -> 84.8 us  [on_device(): pl.pallas_call(kernel, out_shape=pltpu.VMEM((4, 1024, 128), F32), in_spec...]
where the time goes in v3:
time: 86.3 us; the launch traced here: 86.2 us
  Pallas kernels  84.8 us (98%)
  local copies, waits for them, and re-layouts  1.32 us (2%)
    pallas_call x1, Pallas kernels, on_device(): pl.pallas_call(kernel, out_shape=pltpu.VMEM((4, 1024, 128), F32), in_spec...  84.8 us

profile of v3, /device:TPU:1, one launch (start us, length us, event | category | flops | bytes accessed | tf_op | source)
XLA Modules:
  0.0 86.2 jit_solution(5022931725024444623)
XLA Ops:
  0.0 84.8 %shard_map.46 = f32[4,1024,128]{2,1,0:T(8,128)S(1)} custom-call(s32[4,512,128]{2,1,0:T(8,128)} %bitcast.16, s32[4,512,128]{2,1,0:T(8,128)} %bitcast.17, bf16[11,256,256]{2,1,0:T(8,128)(2,1)} %constant.4.clone.mats_hbm, f32[20,128,128]{2,1,0:T(8,128)} %constant.5.clone.vecs_hbm), custom_call_target="tpu_custom_call" | custom-call | tf_op jit(solution)/shard_map/pallas_call | solution.py:409
  84.8 1.3 %copy.6 = f32[32,16384]{1,0:T(8,128)} copy(f32[32,16384]{1,0:T(8,128)S(1)} %bitcast.15) | data formatting | bytes 4194304

commit v4 on v3

--- a/solution.py
+++ b/solution.py
@@ -200,12 +200,12 @@
             device_id_type=MESH,
         ).start()
 
-    def scatter(src, dst, first, count, send_sem, recv_sem):
+    def scatter(src, dst, first, count, send_sem, recv_sem, places=PEERS):
         part = pl.ds(first, count)
         own = pl.ds(me, 1)
         pltpu.make_async_copy(src.at[part, :, own], dst.at[part, :, own], recv_sem).start()
 
-        for place in PEERS:
+        for place in places:
             send(src, dst, part, place, send_sem, recv_sem)
 
     def arrived(src, dst, first, count, recv_sem):
@@ -355,7 +355,7 @@
                 back[first + i, 0] = f[:128, 128 * i : 128 * i + 128]
                 back[first + i, 1] = f[128:, 128 * i : 128 * i + 128]
             scatter(back, home, first, 2, send_i, recv_i.at[4 * h + 2 * g])
-            scatter(back, home, first + 2, 2, send_i, recv_i.at[4 * h + 2 * g + 1])
+            scatter(back, home, first + 2, 2, send_i, recv_i.at[4 * h + 2 * g + 1], sorted(PEERS, key=lambda d: -hops(d)))
             return 0
 
         lax.fori_loop(0, 2, devices_back, 0)

time: 86.3 us -> 85.3 us (0.988)
  Pallas kernels: 84.8 us -> 83.8 us
    pallas_call x1, Pallas kernels: 84.8 us -> 83.8 us  [on_device(): pl.pallas_call(kernel, out_shape=pltpu.VMEM((4, 1024, 128), F32), in_spec...]
where the time goes in v4:
time: 85.3 us; the launch traced here: 85.2 us
  Pallas kernels  83.8 us (98%)
  local copies, waits for them, and re-layouts  1.32 us (2%)
    pallas_call x1, Pallas kernels, on_device(): pl.pallas_call(kernel, out_shape=pltpu.VMEM((4, 1024, 128), F32), in_spec...  83.8 us

profile of v4, /device:TPU:1, one launch (start us, length us, event | category | flops | bytes accessed | tf_op | source)
XLA Modules:
  0.0 85.2 jit_solution(7129492146357471925)
XLA Ops:
  0.0 83.8 %shard_map.46 = f32[4,1024,128]{2,1,0:T(8,128)S(1)} custom-call(s32[4,512,128]{2,1,0:T(8,128)} %bitcast.16, s32[4,512,128]{2,1,0:T(8,128)} %bitcast.17, bf16[11,256,256]{2,1,0:T(8,128)(2,1)} %constant.4.clone.mats_hbm, f32[20,128,128]{2,1,0:T(8,128)} %constant.5.clone.vecs_hbm), custom_call_target="tpu_custom_call" | custom-call | tf_op jit(solution)/shard_map/pallas_call | solution.py:409
  83.9 1.3 %copy.6 = f32[32,16384]{1,0:T(8,128)} copy(f32[32,16384]{1,0:T(8,128)S(1)} %bitcast.15) | data formatting | bytes 4194304
